TPU v7x, 256 devices: a whole 4x4x8 slice. The times are simulated.
256 devices in a mesh: dp: 32 (over x, y, core), tensor: 8 (over z).
Axes of the slice: x: 4, y: 4, z: 8, core: 2. Of those that a mesh axis runs over, the one named last changes fastest.
Arguments:
- activations: bfloat16 [32, 256, 3072], P('dp', None, 'tensor')
- out_grads: bfloat16 [32, 256, 5120], P('dp', 'tensor')
- error_buffer: bfloat16 [32, 3072, 5120], P('dp', 'tensor'), may hold values from -4 to 4
- warm_factor: float32 [5120, 4], replicated, may hold values from -6 to 6
Outputs:
- rebuilt_grad: bfloat16 [3072, 5120], P('tensor')
- next_error: bfloat16 [32, 3072, 5120], P('dp', 'tensor')
- next_factor: float32 [5120, 4], replicated
All inputs are finite; a program needn't handle non-finite values.
Results may differ from a plain program's by a relative error of at most 0.00105.
Values may be sent and summed in bfloat16 or wider, within the bound.
A program may use at most 64 MiB of HBM per device.

v0:
```python
import jax
import jax.numpy as jnp
from jax import lax
from jax.sharding import PartitionSpec as P


def per_device(activations, out_grads, error_buffer, warm_factor):
    high = lax.Precision.HIGHEST
    local_acts = activations[0]
    replicas = lax.axis_size("dp")
    grad = lax.dot_general(
        local_acts,
        lax.all_gather(out_grads, "tensor", axis=1, tiled=True)[0],
        (((0,), (0,)), ((), ())),
        preferred_element_type=jnp.float32,
    )
    matrix = grad + error_buffer[0].astype(jnp.float32)
    left_part = jnp.dot(matrix, warm_factor, precision=high)
    left_mean = lax.psum(left_part, "dp") / replicas
    gram = lax.psum(jnp.dot(left_mean.T, left_mean, precision=high), "tensor")
    lower = jnp.linalg.cholesky(gram)
    left_ortho = lax.linalg.triangular_solve(
        lower, left_mean, left_side=False, lower=True, transpose_a=True
    )
    right_part = jnp.dot(matrix.T, left_ortho, precision=high)
    next_factor = lax.psum(right_part, ("dp", "tensor")) / replicas
    rebuilt = jnp.dot(left_ortho, next_factor.T, precision=high)
    next_error = (matrix - rebuilt).astype(jnp.bfloat16)[None]
    return (rebuilt.astype(jnp.bfloat16), next_error, next_factor)


def solution(mesh):
    return jax.shard_map(
        per_device,
        mesh=mesh,
        in_specs=(P("dp", None, "tensor"), P("dp", "tensor", None), P("dp", "tensor", None), P()),
        out_specs=(P("tensor", None), P("dp", "tensor", None), P()),
        check_vma=False,
    )
```

profile of v0, /device:TPU:32, one launch (start us, length us, event | category | flops | bytes accessed | tf_op | source)
XLA Modules:
  0.0 412.5 jit_solution(14335269687199072824)
XLA Ops:
  7.2 0.0 copy-start
  7.2 0.0 copy-start.3
  7.2 0.0 all-gather.2.cloned.1.call-start
  7.2 0.7 all-gather.2.cloned.1.call-update
  7.9 0.0 all-reduce.2.cloned.1.call-start
  8.0 46.6 %all-gather.2.cloned.1.call-done = bf16[1,256,5120]{2,1,0:T(8,128)(2,1)} async-done(((bf16[1,32,5120]{2,1,0:T(8,128)(2,1)}), bf16[1,256,5120]{2,1,0:T(8,128)(2,1)}) %all-gather.2.cloned.1.call-update) | async-done | bytes 2621456 | tf_op jit(solution)/shard_map/all_gather | solution.py:13
  54.6 0.0 copy-done
  54.6 4.1 %convert_add_fusion = f32[384,5120]{1,0:T(8,128)S(1)} fusion(bf16[1,384,5120]{2,1,0:T(8,128)(2,1)} %param.6, bf16[1,256,5120]{2,1,0:T(8,128)(2,1)} %all-gather.2.cloned.1.call-done, bf16[1,256,384]{2,1,0:T(8,128)(2,1)S(1)} %copy-done), kind=kOutput, calls=%fused_computation | convolution fusion | flops 1010565120 | bytes 14614528 | tf_op jit(solution)/shard_map/dot_general | solution.py:11
  58.8 0.0 copy-start.1
  58.8 3.1 copy-done.1
  61.8 0.0 copy-done.3
  61.8 6.5 %fusion.14 = f32[384,4]{0,1:T(4,128)S(1)} fusion(f32[384,5120]{1,0:T(8,128)S(1)} %convert_add_fusion, f32[5120,4]{0,1:T(4,128)S(1)} %copy-done.3), kind=kOutput, calls=%fused_computation.23 | convolution fusion | flops 94371840 | bytes 7952384 | tf_op jit(solution)/shard_map/dot_general | solution.py:18
  68.3 65.1 %psum.21 = f32[384,4]{0,1:T(4,128)S(1)} all-reduce(f32[384,4]{0,1:T(4,128)S(1)} %fusion.14), channel_id=1, replica_groups=mesh['dp'=32,'tensor'=8] {'dp'}, use_global_device_ids=true, to_apply=%region_0.0 | all-reduce | flops 1536 | bytes 12288 | tf_op jit(solution)/shard_map/psum | solution.py:19
  133.4 0.1 fusion.5
  133.5 14.9 %psum.22 = f32[4,4]{0,1:T(4,128)S(1)} all-reduce(f32[4,4]{0,1:T(4,128)S(1)} %fusion.5), channel_id=1, replica_groups=mesh['dp'=32,'tensor'=8] {'tensor'}, use_global_device_ids=true, to_apply=%region_1.0 | all-reduce | flops 16 | bytes 128 | tf_op jit(solution)/shard_map/psum | solution.py:20
  148.4 0.1 copy.8
  148.5 0.4 cholesky.16
  148.9 0.6 compare_reduce_fusion
  149.6 0.6 fusion.9
  150.2 0.3 custom-call.6
  150.6 0.2 fusion.3
  150.8 8.7 %fusion.15 = f32[5120,4]{0,1:T(4,128)} fusion(f32[384,5120]{1,0:T(8,128)} %copy-done.1, f32[384,4]{0,1:T(4,128)S(1)} %fusion.3), kind=kOutput, calls=%fused_computation.24 | convolution fusion | flops 94371840 | bytes 7952384 | tf_op jit(solution)/shard_map/dot_general | solution.py:25
  159.5 0.0 all-reduce.2.cloned.1.call-update
  159.5 234.4 %all-reduce.2.cloned.1.call-done = f32[5120,4]{0,1:T(4,128)} async-done(((f32[5120,4]{0,1:T(4,128)}), f32[5120,4]{0,1:T(4,128)}) %all-reduce.2.cloned.1.call-update) | async-done | bytes 81936 | tf_op jit(solution)/shard_map/psum | solution.py:26
  394.0 0.9 broadcast_multiply_fusion
  394.9 0.0 copy-start.2
  394.9 10.8 %fusion = (bf16[1,384,5120]{2,1,0:T(8,128)(2,1)}, bf16[384,5120]{1,0:T(8,128)(2,1)}) fusion(f32[384,5120]{1,0:T(8,128)} %copy-done.1, f32[384,4]{0,1:T(4,128)S(1)} %fusion.3, f32[5120,4]{0,1:T(4,128)S(1)} %broadcast_multiply_fusion), kind=kOutput, calls=%fused_computation.2 | convolution fusion | flops 100270080 | bytes 15816704 | tf_op jit(solution)/shard_map/dot_general | solution.py:27
  405.7 0.0 copy-done.2
  (2 shorter events, 0.0 us)
Async XLA Ops:
  7.2 47.5 %copy-start = (bf16[1,256,384]{2,1,0:T(8,128)(2,1)S(1)}, bf16[1,256,384]{2,1,0:T(8,128)(2,1)}, u32[]{:S(2)}) copy-start(bf16[1,256,384]{2,1,0:T(8,128)(2,1)} %param.4) | copy-start | bytes 589828
  7.2 54.7 %copy-start.3 = (f32[5120,4]{0,1:T(4,128)S(1)}, f32[5120,4]{0,1:T(4,128)}, u32[]{:S(2)}) copy-start(f32[5120,4]{0,1:T(4,128)} %param.7) | copy-start | bytes 245764
  7.2 47.4 %all-gather.2.cloned.1.call-start = ((), (), s32[]{:S(2)}) async-start(), calls=%async_computation | async-start | bytes 2949120 | tf_op jit(solution)/shard_map/all_gather | solution.py:13
  7.9 386.0 %all-reduce.2.cloned.1.call-start = ((), (), s32[]{:S(2)}) async-start(), calls=%async_computation.1 | async-start | bytes 163840 | tf_op jit(solution)/shard_map/psum | solution.py:26
  58.8 3.1 copy-start.1
  394.9 10.8 %copy-start.2 = (f32[5120,4]{0,1:T(4,128)}, f32[5120,4]{0,1:T(4,128)S(1)}, u32[]{:S(2)}) copy-start(f32[5120,4]{0,1:T(4,128)S(1)} %broadcast_multiply_fusion) | copy-start | bytes 245764
Sparse Core Ops, SparseCore 0:
  9.8 44.7 all-gather.1
  159.7 234.2 all-reduce.1
where the time goes:
time: 416 us; the launch traced here: 413 us
  waiting for transfers between devices  282 us (68%)
  blocking collectives  80 us (19%)
  matrix products  30.5 us (7%)
  between operations  14.1 us (3%)
    psum x1, waiting for transfers between devices, per_device(): next_factor = lax.psum(right_part, ('dp', 'tensor')) / replicas  234 us
    psum x1, blocking collectives, per_device(): left_mean = lax.psum(left_part, 'dp') / replicas  65.1 us
    all_gather x1, waiting for transfers between devices, per_device(): lax.all_gather(out_grads, 'tensor', axis=1, tiled=True)[0]  46.6 us
    psum x1, blocking collectives, per_device(): gram = lax.psum(jnp.dot(left_mean.T, left_mean, precision=high), 'tensor')  14.9 us
    dot_general x1, matrix products, per_device(): rebuilt = jnp.dot(left_ortho, next_factor.T, precision=high)  10.8 us
    dot_general x1, matrix products, per_device(): right_part = jnp.dot(matrix.T, left_ortho, precision=high)  8.73 us
  transfers between devices with their start and end apart: 2, of which 2 were waited for; matrix products, arithmetic and copies ran while one was open for 0% of the time, Pallas kernels for 0%

commit v1 on v0

v1 whole, which is shorter than its diff:
```python
import functools

import jax
import jax.numpy as jnp
from jax import lax
from jax.experimental import pallas as pl
from jax.experimental.pallas import tpu as pltpu
from jax.sharding import PartitionSpec as P

MESH = pl.DeviceIdType.MESH
F32 = jnp.float32
BF = jnp.bfloat16
DP = 32
NZ = 8
COLS = 640
NN = (((1,), (0,)), ((), ()))
NT = (((1,), (1,)), ((), ()))
TN = (((0,), (0,)), ((), ()))

RIGHT_HOPS = {0: 3, 1: 4, 2: 4, 3: 4, 4: 4, 5: 3, 6: 3, 7: 3}
RIGHT_FIRST = (4, 3, 2, 1)
RIGHT_REST = (0, 7, 6, 5)
LEFT_FIRST = (5, 6, 7)
LEFT_REST = (0, 1, 2, 3, 4)


def hops(direction, k):
    return RIGHT_HOPS[k] if direction == 0 else 7 - RIGHT_HOPS[k]


def dot(a, b, dims):
    return lax.dot_general(a, b, dims, preferred_element_type=F32)


def split16(x):
    r = jnp.concatenate([x, x, x, x], axis=0)
    high = r.astype(BF).astype(F32)
    rest = r - high
    middle = rest.astype(BF).astype(F32)
    low = rest - middle
    row = lax.broadcasted_iota(jnp.int32, r.shape, 0)
    out = jnp.where(row < 4, high, jnp.where(row < 8, middle, jnp.where(row < 12, low, 0.0)))
    return out.astype(BF)


def fold(x):
    return x[0:4] + x[4:8] + x[8:12]


def parts3(x):
    high = x.astype(BF).astype(F32)
    rest = x - high
    middle = rest.astype(BF).astype(F32)
    return high, middle, rest - middle


def chain_kernel(a_hbm, g_hbm, e_hbm, w_hbm, m_ref, nx_ref, lx_ref,
                 a_ref, e_ref, w_ref, g_all, we_ref,
                 p_send, p_buf, l_send, l_buf, z_send, z_buf, r_send, r_buf, n_send, n_buf,
                 load_sem, g_ssem, g_rsem, z_ssem, z_rsem, d_ssem, d_rsem):
    t = lax.axis_index("tensor")
    r = lax.axis_index("dp")
    right, left = lax.rem(t + 1, NZ), lax.rem(t + NZ - 1, NZ)

    barrier = pltpu.get_barrier_semaphore()
    for k in (4, 5, 3, 6, 2, 7, 1):
        pl.semaphore_signal(barrier, inc=1, device_id={"tensor": lax.rem(t + k, NZ)}, device_id_type=MESH)

    def greet(k, carry):
        pl.semaphore_signal(barrier, inc=1, device_id={"dp": lax.rem(r + k, DP)}, device_id_type=MESH)
        return carry

    load_g = pltpu.make_async_copy(g_hbm, g_all.at[pl.ds(pl.multiple_of(t * 32, 32), 32)], load_sem.at[0])
    load_w = pltpu.make_async_copy(w_hbm, w_ref, load_sem.at[1])
    load_a = pltpu.make_async_copy(a_hbm, a_ref, load_sem.at[2])
    load_e = pltpu.make_async_copy(e_hbm, e_ref, load_sem.at[3])
    for c in (load_g, load_w, load_e, load_a):
        c.start()
    lax.fori_loop(1, DP, greet, 0, unroll=True)

    def g_copy(d, s, k):
        origin = lax.rem(t + NZ - s, NZ) if d == 0 else lax.rem(t + s, NZ)
        return _g_copy(origin, d, s, k)

    def _g_copy(origin, d, s, k):
        col = pl.multiple_of(lax.rem(origin + k, NZ) * COLS, COLS)
        ref = g_all.at[pl.ds(pl.multiple_of(origin * 32, 32), 32), pl.ds(col, COLS)]
        return pltpu.make_async_remote_copy(
            ref, ref, g_ssem.at[d, s, k], g_rsem.at[d, s, k],
            device_id={"tensor": (right, left)[d]}, device_id_type=MESH)

    def g_recv(d, s, k):
        if s >= hops(d, k):
            return
        origin = lax.rem(t + NZ - s - 1, NZ) if d == 0 else lax.rem(t + s + 1, NZ)
        _g_copy(origin, d, s, k).wait_recv()
        if s + 1 < hops(d, k):
            _g_copy(origin, d, s + 1, k).start()

    def z_exchange(i, send_of, buf):
        for k in (4, 5, 3, 6, 2, 7, 1):
            to = lax.rem(t + k, NZ)
            pltpu.make_async_remote_copy(send_of(to), buf.at[t], z_ssem.at[i], z_rsem.at[i],
                                         device_id={"tensor": to}, device_id_type=MESH).start()

    def z_wait(i, buf):
        w = buf.at[pl.ds(0, NZ - 1)]
        pltpu.make_async_copy(w, w, z_rsem.at[i]).wait()

    def dp_exchange(i, send, buf):
        def one(k, carry):
            pltpu.make_async_remote_copy(send, buf.at[r], d_ssem.at[i], d_rsem.at[i],
                                         device_id={"dp": lax.rem(r + k, DP)}, device_id_type=MESH).start()
            return carry
        lax.fori_loop(1, DP, one, 0, unroll=True)

    def dp_wait(i, buf):
        w = buf.at[pl.ds(0, DP - 1)]
        pltpu.make_async_copy(w, w, d_rsem.at[i]).wait()

    load_w.wait()
    we_ref[...] = split16(w_ref[...])
    load_g.wait()
    g_own = g_all[pl.ds(pl.multiple_of(t * 32, 32), 32), :]
    p = fold(dot(we_ref[...], g_own, NT))
    wide = jnp.concatenate([p] * NZ, axis=1)
    lane = lax.broadcasted_iota(jnp.int32, (4, 256), 1)
    wide = jnp.where(lane // 32 == t, wide, 0.0)
    p_send[...] = wide
    p_buf[t] = wide

    pl.semaphore_wait(barrier, DP - 1 + NZ - 1)

    z_exchange(0, lambda to: p_send, p_buf)
    for k in RIGHT_FIRST:
        g_copy(0, 0, k).start()
    for k in LEFT_FIRST:
        g_copy(1, 0, k).start()

    load_e.wait()
    left_e = jnp.zeros((16, 384), F32)
    for c in range(NZ):
        cols = pl.ds(c * COLS, COLS)
        left_e = left_e + dot(we_ref[:, cols], e_ref[:, cols], NT)
    load_a.wait()

    for k in RIGHT_FIRST:
        g_recv(0, 0, k)
    for k in LEFT_FIRST:
        g_recv(1, 0, k)
    for k in RIGHT_REST:
        g_copy(0, 0, k).start()
    for k in LEFT_REST:
        g_copy(1, 0, k).start()

    z_wait(0, p_buf)
    p_all = p_buf[0]
    for i in range(1, NZ):
        p_all = p_all + p_buf[i]
    left_part = fold(left_e) + fold(dot(split16(p_all), a_ref[...], NN))
    l_send[...] = left_part
    l_buf[r] = left_part
    dp_exchange(0, l_send, l_buf)

    for s in (1, 2):
        for k in RIGHT_FIRST:
            if k > s:
                g_recv(0, s, k)
        for k in LEFT_FIRST:
            if 8 - k > s:
                g_recv(1, s, k)

    dp_wait(0, l_buf)
    lm = l_buf[0]
    for i in range(1, DP):
        lm = lm + l_buf[i]
    lm = lm * (1.0 / DP)
    peak = jnp.maximum(jnp.max(jnp.max(jnp.abs(lm), axis=1, keepdims=True), axis=0, keepdims=True), 1e-30)
    lm = lm / peak
    l16 = split16(lm)
    gram = fold(dot(l16, l16, NT))
    gram = gram[:, 0:4] + gram[:, 4:8] + gram[:, 8:12]
    info = jnp.concatenate([gram, jnp.broadcast_to(peak, (4, 124))], axis=1)
    q = fold(dot(l16, a_ref[...], NT))
    for c in range(NZ):
        z_send[c, :, 640:896] = q
        z_send[c, :, 896:1024] = info
        z_send[c, :, 0:640] = fold(dot(l16, e_ref[:, c * COLS:(c + 1) * COLS], NN))
    z_exchange(1, lambda to: z_send.at[to], z_buf)
    z_buf[t] = z_send[t]

    for k in (4,):
        g_recv(0, 3, k)

    z_wait(1, z_buf)
    peaks = [z_buf[i, :, 1000:1001] for i in range(NZ)]
    top = peaks[0]
    for i in range(1, NZ):
        top = jnp.maximum(top, peaks[i])
    scales = [x / top for x in peaks]
    total = z_buf[0, :, 0:896] * scales[0]
    gram = z_buf[0, :, 896:900] * (scales[0] * scales[0])
    for i in range(1, NZ):
        total = total + z_buf[i, :, 0:896] * scales[i]
        gram = gram + z_buf[i, :, 896:900] * (scales[i] * scales[i])
    mine = pl.ds(pl.multiple_of(t * COLS, COLS), COLS)
    right_part = total[:, 0:640] + fold(dot(split16(total[:, 640:896]), g_all[:, mine], NN))
    r_send[...] = right_part
    r_buf[r] = right_part
    dp_exchange(1, r_send, r_buf)

    lower = [[None] * 4 for _ in range(4)]
    for i in range(4):
        for j in range(i + 1):
            v = gram[i:i + 1, j:j + 1]
            for k in range(j):
                v = v - lower[i][k] * lower[j][k]
            lower[i][j] = jnp.sqrt(v) if i == j else v / lower[j][j]

    def solve(rows):
        out = []
        for j in range(4):
            v = rows[j]
            for i in range(j):
                v = v - out[i] * lower[j][i]
            out.append(v / lower[j][j])
        return jnp.concatenate(out, axis=0)

    own_scale = peak / top[0:1]
    lm = lm * own_scale
    lo = solve([lm[j:j + 1] for j in range(4)])
    high, middle, low = parts3(lo)
    zero = jnp.zeros_like(lo)
    lx_ref[...] = jnp.concatenate([high, high, middle, middle, high, low, zero, zero], axis=0).astype(BF)

    rest = [(d, s, k) for s in range(4) for d, k in
            [(0, k) for k in RIGHT_FIRST + RIGHT_REST] + [(1, k) for k in LEFT_FIRST + LEFT_REST]]
    done = {(0, 0, k) for k in RIGHT_FIRST} | {(1, 0, k) for k in LEFT_FIRST}
    done |= {(0, s, k) for s in (1, 2) for k in RIGHT_FIRST if k > s}
    done |= {(1, s, k) for s in (1, 2) for k in LEFT_FIRST if 8 - k > s}
    done |= {(0, 3, 4)}
    rest = [x for x in rest if x not in done]
    for x in rest[:14]:
        g_recv(*x)

    dp_wait(1, r_buf)
    nr = r_buf[0]
    for i in range(1, DP):
        nr = nr + r_buf[i]
    nr = nr * (1.0 / DP)
    n_send[...] = nr
    n_buf[t] = nr
    z_exchange(2, lambda to: n_send, n_buf)

    for x in rest[14:]:
        g_recv(*x)

    at = jnp.transpose(a_ref[...])
    for c in range(NZ):
        cols = slice(c * COLS, (c + 1) * COLS)
        m_ref[:, cols] = dot(at, g_all[:, cols], NN) + e_ref[:, cols].astype(F32)

    z_wait(2, n_buf)
    for c in range(NZ):
        x = n_buf[c]
        nx_ref[:, c * COLS:(c + 1) * COLS] = solve([x[j:j + 1] for j in range(4)])

    for d in range(2):
        for k in range(NZ):
            for s in range(hops(d, k)):
                g_copy(d, s, k).wait_send()
    for i, buf in enumerate((p_buf, z_buf, n_buf)):
        w = buf.at[pl.ds(0, NZ - 1)]
        pltpu.make_async_copy(w, w, z_ssem.at[i]).wait()
    for i, buf in enumerate((l_buf, r_buf)):
        w = buf.at[pl.ds(0, DP - 1)]
        pltpu.make_async_copy(w, w, d_ssem.at[i]).wait()


def finish_kernel(m_ref, n_ref, lx_ref, rebuilt_hbm, error_hbm, nout_ref, out_a, out_b, sem):
    lxt = lx_ref[...]
    nout_ref[...] = n_ref[...]
    copies = []
    for c in range(NZ):
        cols = slice(c * COLS, (c + 1) * COLS)
        high, middle, low = parts3(n_ref[:, cols])
        zero = jnp.zeros_like(high)
        nx = jnp.concatenate([high, middle, high, middle, low, high, zero, zero], axis=0).astype(BF)
        rebuilt = dot(lxt, nx, TN)
        out_a[:, cols] = rebuilt.astype(BF)
        out_b[:, cols] = (m_ref[:, cols] - rebuilt).astype(BF)
        for i, (src, dst) in enumerate(((out_a, rebuilt_hbm), (out_b, error_hbm))):
            cp = pltpu.make_async_copy(src.at[:, cols], dst.at[:, cols], sem.at[i, c])
            cp.start()
            copies.append(cp)
    for cp in copies:
        cp.wait()


def per_device(activations, out_grads, error_buffer, warm_factor):
    any_spec = pl.BlockSpec(memory_space=pl.ANY)
    vmem = pl.BlockSpec(memory_space=pltpu.VMEM)
    V = pltpu.VMEM
    D = pltpu.SemaphoreType.DMA
    m, n, lx = pl.pallas_call(
        chain_kernel,
        out_shape=OUT_SHAPES(),
        in_specs=[any_spec] * 4,
        out_specs=[vmem] * 3,
        scratch_shapes=[
            V((256, 384), BF), V((384, 5120), BF), V((4, 5120), F32), V((256, 5120), BF), V((16, 5120), BF),
            V((4, 256), F32), V((NZ, 4, 256), F32), V((4, 384), F32), V((DP, 4, 384), F32),
            V((NZ, 4, 1024), F32), V((NZ, 4, 1024), F32), V((4, 640), F32), V((DP, 4, 640), F32),
            V((4, 640), F32), V((NZ, 4, 640), F32),
            D((4,)), D((2, 4, NZ)), D((2, 4, NZ)), D((3,)), D((3,)), D((2,)), D((2,)),
        ],
        compiler_params=pltpu.CompilerParams(collective_id=0, has_side_effects=True, vmem_limit_bytes=32 << 20),
    )(activations[0], out_grads[0], error_buffer[0], warm_factor.T)
    rebuilt, error, factor = pl.pallas_call(
        finish_kernel,
        out_shape=[jax.ShapeDtypeStruct((384, 5120), BF), jax.ShapeDtypeStruct((384, 5120), BF),
                   jax.ShapeDtypeStruct((4, 5120), F32)],
        in_specs=[vmem] * 3,
        out_specs=[any_spec, any_spec, vmem],
        scratch_shapes=[V((384, 5120), BF), V((384, 5120), BF), D((2, NZ))],
        compiler_params=pltpu.CompilerParams(vmem_limit_bytes=32 << 20),
    )(m, n, lx)
    return rebuilt, error[None], factor.T


def OUT_SHAPES():
    return [jax.ShapeDtypeStruct((384, 5120), F32), jax.ShapeDtypeStruct((4, 5120), F32),
            jax.ShapeDtypeStruct((32, 384), BF)]


def solution(mesh):
    return jax.shard_map(
        per_device,
        mesh=mesh,
        in_specs=(P("dp", None, "tensor"), P("dp", "tensor", None), P("dp", "tensor", None), P()),
        out_specs=(P("tensor", None), P("dp", "tensor", None), P()),
        check_vma=False,
    )
```

time: 416 us -> 62.4 us (0.15)
  waiting for transfers between devices: 282 us -> 0 us
  blocking collectives: 80 us -> 0 us
  Pallas kernels: 0 us -> 56.1 us
  matrix products: 30.5 us -> 0 us
  between operations: 14.1 us -> 0.65 us
    psum x1 -> x0, waiting for transfers between devices: 234 us -> none  [per_device(): next_factor = lax.psum(right_part, ('dp', 'tensor')) / replicas]
    psum x2 -> x0, blocking collectives: 80 us -> none  [the longest x1 65.1 us: per_device(): left_mean = lax.psum(left_part, 'dp') / replicas]
    pallas_call x0 -> x2, Pallas kernels: none -> 56.1 us  [the longest x1 51.8 us: per_device(): pl.pallas_call(chain_kernel, out_shape=OUT_SHAPES(), in_specs=[any_spec]...]
    all_gather x1 -> x0, waiting for transfers between devices: 46.6 us -> none  [per_device(): lax.all_gather(out_grads, 'tensor', axis=1, tiled=True)[0]]
    dot_general x5 -> x0, matrix products: 30.3 us -> none  [the longest x1 10.8 us: per_device(): rebuilt = jnp.dot(left_ortho, next_factor.T, precision=high)]
  transfers between devices with their start and end apart: 2 -> 0, of which waited for: 2 -> 0; matrix products, arithmetic and copies ran while one was open for 0% -> 0% of each run, Pallas kernels for 0% -> 0%
where the time goes in v1:
time: 62.4 us; the launch traced here: 61.6 us
  Pallas kernels  56.1 us (90%)
  local copies, waits for them, and re-layouts  4.89 us (8%)
  between operations  0.65 us (1%)
    pallas_call x1, Pallas kernels, per_device(): pl.pallas_call(chain_kernel, out_shape=OUT_SHAPES(), in_specs=[any_spec]...  51.8 us
    unnamed x8, local copies, waits for them, and re-layouts  4.89 us
    pallas_call x1, Pallas kernels, per_device(): pl.pallas_call(finish_kernel, out_shape=[jax.ShapeDtypeStruct((384, 5120)...  4.25 us

profile of v1, /device:TPU:32, one launch (start us, length us, event | category | flops | bytes accessed | tf_op | source)
XLA Modules:
  0.0 61.6 jit_solution(16622729719983096568)
XLA Ops:
  0.6 0.0 copy-start
  0.6 2.1 %copy-done = bf16[1,384,5120]{2,1,0:T(8,128)(2,1)S(1)} copy-done((bf16[1,384,5120]{2,1,0:T(8,128)(2,1)S(1)}, bf16[1,384,5120]{2,1,0:T(8,128)(2,1)}, u32[]{:S(2)}) %copy-start) | copy-done | bytes 3932184
  2.7 0.0 copy-start.1
  2.7 1.0 %copy-done.1 = bf16[1,32,5120]{2,1,0:T(8,128)(2,1)S(1)} copy-done((bf16[1,32,5120]{2,1,0:T(8,128)(2,1)S(1)}, bf16[1,32,5120]{2,1,0:T(8,128)(2,1)}, u32[]{:S(2)}) %copy-start.1) | copy-done | bytes 327704
  3.7 0.0 copy-start.2
  3.7 0.9 %copy-done.2 = bf16[1,256,384]{2,1,0:T(8,128)(2,1)S(1)} copy-done((bf16[1,256,384]{2,1,0:T(8,128)(2,1)S(1)}, bf16[1,256,384]{2,1,0:T(8,128)(2,1)}, u32[]{:S(2)}) %copy-start.2) | copy-done | bytes 196632
  4.6 0.0 copy-start.3
  4.6 0.9 %copy-done.3 = f32[5120,4]{0,1:T(4,128)S(1)} copy-done((f32[5120,4]{0,1:T(4,128)S(1)}, f32[5120,4]{0,1:T(4,128)}, u32[]{:S(2)}) %copy-start.3) | copy-done | bytes 81944
  5.5 51.8 %shard_map.67 = (f32[384,5120]{1,0:T(8,128)S(1)}, f32[4,5120]{1,0:T(4,128)S(1)}, bf16[32,384]{1,0:T(8,128)(2,1)S(1)}) custom-call(bf16[256,384]{1,0:T(8,128)(2,1)S(1)} %bitcast.8, bf16[32,5120]{1,0:T(8,128)(2,1)S(1)} %bitcast.7, bf16[384,5120]{1,0:T(8,128)(2,1)S(1)} %bitcast.6, f32[4,5120]{1,0:T(4,128)S(1)} %bitcast.9), custom_call_target="tpu_custom_call" | custom-call | tf_op jit(solution)/shard_map/pallas_call | solution.py:305
  57.4 4.3 %shard_map.68 = (bf16[384,5120]{1,0:T(8,128)(2,1)}, bf16[384,5120]{1,0:T(8,128)(2,1)}, f32[4,5120]{1,0:T(4,128)}) custom-call(f32[384,5120]{1,0:T(8,128)S(1)} %get-tuple-element.9.m_ref, f32[4,5120]{1,0:T(4,128)S(1)} %get-tuple-element.10.n_ref, bf16[32,384]{1,0:T(8,128)(2,1)S(1)} %get-tuple-element.11.lx_ref), custom_call_target="tpu_custom_call" | custom-call | tf_op jit(solution)/shard_map/pallas_call | solution.py:319
Async XLA Ops:
  0.6 2.1 %copy-start = (bf16[1,384,5120]{2,1,0:T(8,128)(2,1)S(1)}, bf16[1,384,5120]{2,1,0:T(8,128)(2,1)}, u32[]{:S(2)}) copy-start(bf16[1,384,5120]{2,1,0:T(8,128)(2,1)} %param.6) | copy-start | bytes 11796484
  2.7 1.0 %copy-start.1 = (bf16[1,32,5120]{2,1,0:T(8,128)(2,1)S(1)}, bf16[1,32,5120]{2,1,0:T(8,128)(2,1)}, u32[]{:S(2)}) copy-start(bf16[1,32,5120]{2,1,0:T(8,128)(2,1)} %param.5) | copy-start | bytes 983044
  3.7 0.9 %copy-start.2 = (bf16[1,256,384]{2,1,0:T(8,128)(2,1)S(1)}, bf16[1,256,384]{2,1,0:T(8,128)(2,1)}, u32[]{:S(2)}) copy-start(bf16[1,256,384]{2,1,0:T(8,128)(2,1)} %param.4) | copy-start | bytes 589828
  4.6 0.9 %copy-start.3 = (f32[5120,4]{0,1:T(4,128)S(1)}, f32[5120,4]{0,1:T(4,128)}, u32[]{:S(2)}) copy-start(f32[5120,4]{0,1:T(4,128)} %param.7) | copy-start | bytes 245764

commit v2 on v1

--- a/solution.py
+++ b/solution.py
@@ -18,11 +18,20 @@
 TN = (((0,), (0,)), ((), ()))
 
 RIGHT_HOPS = {0: 3, 1: 4, 2: 4, 3: 4, 4: 4, 5: 3, 6: 3, 7: 3}
-RIGHT_FIRST = (4, 3, 2, 1)
-RIGHT_REST = (0, 7, 6, 5)
-LEFT_FIRST = (5, 6, 7)
-LEFT_REST = (0, 1, 2, 3, 4)
-
+CHIPS = 16
+FAR_FIRST = sorted(((dx, dy) for dx in range(4) for dy in range(4) if dx or dy),
+                   key=lambda v: -(min(v[0], 4 - v[0]) + min(v[1], 4 - v[1])))
+GATHER = {
+    "start": ((0, -1, (4, 3, 2, 1)), (1, -1, (5, 6, 7)), (0, -1, (0, 7)), (1, -1, (0, 4, 3))),
+    "left": ((0, 0, (4, 3)), (1, 0, (5,))),
+    "pair0": ((0, 0, (2,)), (1, 0, (6,)), (0, -1, (6, 5)), (1, -1, (2, 1))),
+    "sent0": ((0, 1, (4, 3)), (1, 1, (5,)), (0, 0, (1, 0)), (1, 0, (7, 0))),
+    "sums": ((0, 2, (4,)), (0, 0, (7, 6, 5)), (1, 0, (4, 3, 2, 1)), (0, 1, (2, 1)), (1, 1, (6, 7))),
+    "mine": ((0, 3, (4,)), (0, 2, (3,)), (1, 2, (5,)), (0, 1, (0,)), (1, 1, (0,))),
+    "pair1": ((0, 1, (7,)), (1, 1, (4,))),
+    "sent1": ((0, 1, (6, 5)), (1, 1, (3, 2, 1)), (0, 2, (2, 1)), (1, 2, (6, 7, 0))),
+    "rest": ((0, 2, (0, 7, 6, 5)), (1, 2, (4, 3, 2, 1)), (0, 3, (3, 2, 1)), (1, 3, (5, 6, 7, 0))),
+}
 
 def hops(direction, k):
     return RIGHT_HOPS[k] if direction == 0 else 7 - RIGHT_HOPS[k]
@@ -56,19 +65,18 @@
 
 def chain_kernel(a_hbm, g_hbm, e_hbm, w_hbm, m_ref, nx_ref, lx_ref,
                  a_ref, e_ref, w_ref, g_all, we_ref,
-                 p_send, p_buf, l_send, l_buf, z_send, z_buf, r_send, r_buf, n_send, n_buf,
-                 load_sem, g_ssem, g_rsem, z_ssem, z_rsem, d_ssem, d_rsem):
+                 p_send, p_buf, l_pair, l_send, l_buf, z_send, z_buf, r_pair, r_send, r_buf, n_send, n_buf,
+                 load_sem, g_ssem, g_rsem, z_ssem, z_rsem, d_ssem, d_rsem, pair_ssem, pair_rsem):
     t = lax.axis_index("tensor")
     r = lax.axis_index("dp")
     right, left = lax.rem(t + 1, NZ), lax.rem(t + NZ - 1, NZ)
+    x, y, core = r // 8, lax.rem(r // 2, 4), lax.rem(r, 2)
+    chip = r // 2
+    sibling = r + 1 - 2 * core
 
     barrier = pltpu.get_barrier_semaphore()
     for k in (4, 5, 3, 6, 2, 7, 1):
         pl.semaphore_signal(barrier, inc=1, device_id={"tensor": lax.rem(t + k, NZ)}, device_id_type=MESH)
-
-    def greet(k, carry):
-        pl.semaphore_signal(barrier, inc=1, device_id={"dp": lax.rem(r + k, DP)}, device_id_type=MESH)
-        return carry
 
     load_g = pltpu.make_async_copy(g_hbm, g_all.at[pl.ds(pl.multiple_of(t * 32, 32), 32)], load_sem.at[0])
     load_w = pltpu.make_async_copy(w_hbm, w_ref, load_sem.at[1])
@@ -76,7 +84,10 @@
     load_e = pltpu.make_async_copy(e_hbm, e_ref, load_sem.at[3])
     for c in (load_g, load_w, load_e, load_a):
         c.start()
-    lax.fori_loop(1, DP, greet, 0, unroll=True)
+    for dx, dy in FAR_FIRST:
+        to = lax.rem(x + dx, 4) * 8 + lax.rem(y + dy, 4) * 2 + core
+        pl.semaphore_signal(barrier, inc=1, device_id={"dp": to}, device_id_type=MESH)
+    pl.semaphore_signal(barrier, inc=1, device_id={"dp": sibling}, device_id_type=MESH)
 
     def g_copy(d, s, k):
         origin = lax.rem(t + NZ - s, NZ) if d == 0 else lax.rem(t + s, NZ)
@@ -97,6 +108,14 @@
         if s + 1 < hops(d, k):
             _g_copy(origin, d, s + 1, k).start()
 
+    def gather(point):
+        for d, s, chunks in GATHER[point]:
+            for k in chunks:
+                if s < 0:
+                    g_copy(d, 0, k).start()
+                else:
+                    g_recv(d, s, k)
+
     def z_exchange(i, send_of, buf):
         for k in (4, 5, 3, 6, 2, 7, 1):
             to = lax.rem(t + k, NZ)
@@ -107,15 +126,18 @@
         w = buf.at[pl.ds(0, NZ - 1)]
         pltpu.make_async_copy(w, w, z_rsem.at[i]).wait()
 
+    def pair_copy(i, send, buf):
+        return pltpu.make_async_remote_copy(send, buf, pair_ssem.at[i], pair_rsem.at[i],
+                                            device_id={"dp": sibling}, device_id_type=MESH)
+
     def dp_exchange(i, send, buf):
-        def one(k, carry):
-            pltpu.make_async_remote_copy(send, buf.at[r], d_ssem.at[i], d_rsem.at[i],
-                                         device_id={"dp": lax.rem(r + k, DP)}, device_id_type=MESH).start()
-            return carry
-        lax.fori_loop(1, DP, one, 0, unroll=True)
+        for dx, dy in FAR_FIRST:
+            to = lax.rem(x + dx, 4) * 8 + lax.rem(y + dy, 4) * 2 + core
+            pltpu.make_async_remote_copy(send, buf.at[chip], d_ssem.at[i], d_rsem.at[i],
+                                         device_id={"dp": to}, device_id_type=MESH).start()
 
     def dp_wait(i, buf):
-        w = buf.at[pl.ds(0, DP - 1)]
+        w = buf.at[pl.ds(0, CHIPS - 1)]
         pltpu.make_async_copy(w, w, d_rsem.at[i]).wait()
 
     load_w.wait()
@@ -129,13 +151,10 @@
     p_send[...] = wide
     p_buf[t] = wide
 
-    pl.semaphore_wait(barrier, DP - 1 + NZ - 1)
+    pl.semaphore_wait(barrier, CHIPS + NZ - 1)
 
     z_exchange(0, lambda to: p_send, p_buf)
-    for k in RIGHT_FIRST:
-        g_copy(0, 0, k).start()
-    for k in LEFT_FIRST:
-        g_copy(1, 0, k).start()
+    gather("start")
 
     load_e.wait()
     left_e = jnp.zeros((16, 384), F32)
@@ -144,35 +163,26 @@
         left_e = left_e + dot(we_ref[:, cols], e_ref[:, cols], NT)
     load_a.wait()
 
-    for k in RIGHT_FIRST:
-        g_recv(0, 0, k)
-    for k in LEFT_FIRST:
-        g_recv(1, 0, k)
-    for k in RIGHT_REST:
-        g_copy(0, 0, k).start()
-    for k in LEFT_REST:
-        g_copy(1, 0, k).start()
+    gather("left")
 
     z_wait(0, p_buf)
     p_all = p_buf[0]
     for i in range(1, NZ):
         p_all = p_all + p_buf[i]
     left_part = fold(left_e) + fold(dot(split16(p_all), a_ref[...], NN))
+    l_pair[0] = left_part
+    pair_copy(0, l_pair.at[0], l_pair.at[1]).start()
+    gather("pair0")
+    pair_copy(0, l_pair.at[0], l_pair.at[1]).wait_recv()
+    left_part = left_part + l_pair[1]
     l_send[...] = left_part
-    l_buf[r] = left_part
+    l_buf[chip] = left_part
     dp_exchange(0, l_send, l_buf)
-
-    for s in (1, 2):
-        for k in RIGHT_FIRST:
-            if k > s:
-                g_recv(0, s, k)
-        for k in LEFT_FIRST:
-            if 8 - k > s:
-                g_recv(1, s, k)
+    gather("sent0")
 
     dp_wait(0, l_buf)
     lm = l_buf[0]
-    for i in range(1, DP):
+    for i in range(1, CHIPS):
         lm = lm + l_buf[i]
     lm = lm * (1.0 / DP)
     peak = jnp.maximum(jnp.max(jnp.max(jnp.abs(lm), axis=1, keepdims=True), axis=0, keepdims=True), 1e-30)
@@ -189,8 +199,7 @@
     z_exchange(1, lambda to: z_send.at[to], z_buf)
     z_buf[t] = z_send[t]
 
-    for k in (4,):
-        g_recv(0, 3, k)
+    gather("sums")
 
     z_wait(1, z_buf)
     peaks = [z_buf[i, :, 1000:1001] for i in range(NZ)]
@@ -203,10 +212,16 @@
     for i in range(1, NZ):
         total = total + z_buf[i, :, 0:896] * scales[i]
         gram = gram + z_buf[i, :, 896:900] * (scales[i] * scales[i])
+    gather("mine")
     mine = pl.ds(pl.multiple_of(t * COLS, COLS), COLS)
     right_part = total[:, 0:640] + fold(dot(split16(total[:, 640:896]), g_all[:, mine], NN))
+    r_pair[0] = right_part
+    pair_copy(1, r_pair.at[0], r_pair.at[1]).start()
+    gather("pair1")
+    pair_copy(1, r_pair.at[0], r_pair.at[1]).wait_recv()
+    right_part = right_part + r_pair[1]
     r_send[...] = right_part
-    r_buf[r] = right_part
+    r_buf[chip] = right_part
     dp_exchange(1, r_send, r_buf)
 
     lower = [[None] * 4 for _ in range(4)]
@@ -233,27 +248,17 @@
     zero = jnp.zeros_like(lo)
     lx_ref[...] = jnp.concatenate([high, high, middle, middle, high, low, zero, zero], axis=0).astype(BF)
 
-    rest = [(d, s, k) for s in range(4) for d, k in
-            [(0, k) for k in RIGHT_FIRST + RIGHT_REST] + [(1, k) for k in LEFT_FIRST + LEFT_REST]]
-    done = {(0, 0, k) for k in RIGHT_FIRST} | {(1, 0, k) for k in LEFT_FIRST}
-    done |= {(0, s, k) for s in (1, 2) for k in RIGHT_FIRST if k > s}
-    done |= {(1, s, k) for s in (1, 2) for k in LEFT_FIRST if 8 - k > s}
-    done |= {(0, 3, 4)}
-    rest = [x for x in rest if x not in done]
-    for x in rest[:14]:
-        g_recv(*x)
-
+    gather("sent1")
     dp_wait(1, r_buf)
     nr = r_buf[0]
-    for i in range(1, DP):
+    for i in range(1, CHIPS):
         nr = nr + r_buf[i]
     nr = nr * (1.0 / DP)
     n_send[...] = nr
     n_buf[t] = nr
     z_exchange(2, lambda to: n_send, n_buf)
 
-    for x in rest[14:]:
-        g_recv(*x)
+    gather("rest")
 
     at = jnp.transpose(a_ref[...])
     for c in range(NZ):
@@ -272,8 +277,10 @@
     for i, buf in enumerate((p_buf, z_buf, n_buf)):
         w = buf.at[pl.ds(0, NZ - 1)]
         pltpu.make_async_copy(w, w, z_ssem.at[i]).wait()
+    pair_copy(0, l_pair.at[0], l_pair.at[1]).wait_send()
+    pair_copy(1, r_pair.at[0], r_pair.at[1]).wait_send()
     for i, buf in enumerate((l_buf, r_buf)):
-        w = buf.at[pl.ds(0, DP - 1)]
+        w = buf.at[pl.ds(0, CHIPS - 1)]
         pltpu.make_async_copy(w, w, d_ssem.at[i]).wait()
 
 
@@ -299,23 +306,25 @@
 
 def per_device(activations, out_grads, error_buffer, warm_factor):
     any_spec = pl.BlockSpec(memory_space=pl.ANY)
+    hbm_spec = pl.BlockSpec(memory_space=pltpu.HBM)
     vmem = pl.BlockSpec(memory_space=pltpu.VMEM)
     V = pltpu.VMEM
     D = pltpu.SemaphoreType.DMA
     m, n, lx = pl.pallas_call(
         chain_kernel,
         out_shape=OUT_SHAPES(),
-        in_specs=[any_spec] * 4,
+        in_specs=[hbm_spec] * 4,
         out_specs=[vmem] * 3,
         scratch_shapes=[
             V((256, 384), BF), V((384, 5120), BF), V((4, 5120), F32), V((256, 5120), BF), V((16, 5120), BF),
-            V((4, 256), F32), V((NZ, 4, 256), F32), V((4, 384), F32), V((DP, 4, 384), F32),
-            V((NZ, 4, 1024), F32), V((NZ, 4, 1024), F32), V((4, 640), F32), V((DP, 4, 640), F32),
+            V((4, 256), F32), V((NZ, 4, 256), F32), V((2, 4, 384), F32), V((4, 384), F32), V((CHIPS, 4, 384), F32),
+            V((NZ, 4, 1024), F32), V((NZ, 4, 1024), F32), V((2, 4, 640), F32), V((4, 640), F32), V((CHIPS, 4, 640), F32),
             V((4, 640), F32), V((NZ, 4, 640), F32),
-            D((4,)), D((2, 4, NZ)), D((2, 4, NZ)), D((3,)), D((3,)), D((2,)), D((2,)),
+            D((4,)), D((2, 4, NZ)), D((2, 4, NZ)), D((3,)), D((3,)), D((2,)), D((2,)), D((2,)), D((2,)),
         ],
         compiler_params=pltpu.CompilerParams(collective_id=0, has_side_effects=True, vmem_limit_bytes=32 << 20),
-    )(activations[0], out_grads[0], error_buffer[0], warm_factor.T)
+    )(*(pltpu.with_memory_space_constraint(x, pltpu.HBM)
+        for x in (activations[0], out_grads[0], error_buffer[0], warm_factor.T)))
     rebuilt, error, factor = pl.pallas_call(
         finish_kernel,
         out_shape=[jax.ShapeDtypeStruct((384, 5120), BF), jax.ShapeDtypeStruct((384, 5120), BF),

time: 62.4 us -> 48.4 us (0.78); the launches traced: 61.6 us -> 48.3 us
  Pallas kernels: 56.1 us -> 47.7 us
  local copies, waits for them, and re-layouts: 4.89 us -> 0 us
    pallas_call x1, Pallas kernels: 51.8 us -> 43.5 us  [per_device(): pl.pallas_call(chain_kernel, out_shape=OUT_SHAPES(), in_specs=[hbm_spec]...]
    unnamed x8 -> x0, local copies, waits for them, and re-layouts: 4.89 us -> none
where the time goes in v2:
time: 48.4 us; the launch traced here: 48.3 us
  Pallas kernels  47.7 us (99%)
  between operations  0.64 us (1%)
    pallas_call x1, Pallas kernels, per_device(): pl.pallas_call(chain_kernel, out_shape=OUT_SHAPES(), in_specs=[hbm_spec]...  43.5 us
    pallas_call x1, Pallas kernels, per_device(): pl.pallas_call(finish_kernel, out_shape=[jax.ShapeDtypeStruct((384, 5120)...  4.25 us

profile of v2, /device:TPU:32, one launch (start us, length us, event | category | flops | bytes accessed | tf_op | source)
XLA Modules:
  0.0 48.3 jit_solution(3994315156423419019)
XLA Ops:
  0.6 43.5 %shard_map.67 = (f32[384,5120]{1,0:T(8,128)S(1)}, f32[4,5120]{1,0:T(4,128)S(1)}, bf16[32,384]{1,0:T(8,128)(2,1)S(1)}) custom-call(bf16[256,384]{1,0:T(8,128)(2,1)} %bitcast.8, bf16[32,5120]{1,0:T(8,128)(2,1)} %bitcast.7, bf16[384,5120]{1,0:T(8,128)(2,1)} %bitcast.6, f32[4,5120]{1,0:T(4,128)} %bitcast.9), custom_call_target="tpu_custom_call" | custom-call | tf_op jit(solution)/shard_map/pallas_call | solution.py:313
  44.1 4.2 %shard_map.68 = (bf16[384,5120]{1,0:T(8,128)(2,1)}, bf16[384,5120]{1,0:T(8,128)(2,1)}, f32[4,5120]{1,0:T(4,128)}) custom-call(f32[384,5120]{1,0:T(8,128)S(1)} %get-tuple-element.9.m_ref, f32[4,5120]{1,0:T(4,128)S(1)} %get-tuple-element.10.n_ref, bf16[32,384]{1,0:T(8,128)(2,1)S(1)} %get-tuple-element.11.lx_ref), custom_call_target="tpu_custom_call" | custom-call | tf_op jit(solution)/shard_map/pallas_call | solution.py:328

commit v3 on v2

--- a/solution.py
+++ b/solution.py
@@ -22,16 +22,20 @@
 FAR_FIRST = sorted(((dx, dy) for dx in range(4) for dy in range(4) if dx or dy),
                    key=lambda v: -(min(v[0], 4 - v[0]) + min(v[1], 4 - v[1])))
 GATHER = {
-    "start": ((0, -1, (4, 3, 2, 1)), (1, -1, (5, 6, 7)), (0, -1, (0, 7)), (1, -1, (0, 4, 3))),
-    "left": ((0, 0, (4, 3)), (1, 0, (5,))),
-    "pair0": ((0, 0, (2,)), (1, 0, (6,)), (0, -1, (6, 5)), (1, -1, (2, 1))),
-    "sent0": ((0, 1, (4, 3)), (1, 1, (5,)), (0, 0, (1, 0)), (1, 0, (7, 0))),
-    "sums": ((0, 2, (4,)), (0, 0, (7, 6, 5)), (1, 0, (4, 3, 2, 1)), (0, 1, (2, 1)), (1, 1, (6, 7))),
-    "mine": ((0, 3, (4,)), (0, 2, (3,)), (1, 2, (5,)), (0, 1, (0,)), (1, 1, (0,))),
-    "pair1": ((0, 1, (7,)), (1, 1, (4,))),
-    "sent1": ((0, 1, (6, 5)), (1, 1, (3, 2, 1)), (0, 2, (2, 1)), (1, 2, (6, 7, 0))),
-    "rest": ((0, 2, (0, 7, 6, 5)), (1, 2, (4, 3, 2, 1)), (0, 3, (3, 2, 1)), (1, 3, (5, 6, 7, 0))),
+    "start": ((0, -1, (4, 3, 2, 1, )), (1, -1, (5, 6, 7, )), (0, -1, (0, 7, )), (1, -1, (0, 4, 3, ))),
+    "middle": (),
+    "left": ((0, 0, (4, 3, )), (1, 0, (5, ))),
+    "pair0": ((0, 0, (2, )), (1, 0, (6, )), (0, -1, (6, 5, )), (1, -1, (2, 1, ))),
+    "sent0": ((0, 1, (4, 3, )), (1, 1, (5, )), (0, 0, (1, 0, )), (1, 0, (7, 0, ))),
+    "prepare2": (),
+    "prepare4": (),
+    "sums": ((0, 2, (4, )), (0, 0, (7, 6, 5, )), (1, 0, (4, 3, 2, 1, )), (0, 1, (2, 1, )), (1, 1, (6, 7, ))),
+    "mine": ((0, 3, (4, )), (0, 2, (3, )), (1, 2, (5, )), (0, 1, (0, )), (1, 1, (0, ))),
+    "pair1": ((0, 1, (7, )), (1, 1, (4, ))),
+    "sent1": ((0, 1, (6, 5, )), (1, 1, (3, 2, 1, )), (0, 2, (2, 1, )), (1, 2, (6, 7, 0, ))),
+    "rest": ((0, 2, (0, 7, 6, 5, )), (1, 2, (4, 3, 2, 1, ))),
 }
+
 
 def hops(direction, k):
     return RIGHT_HOPS[k] if direction == 0 else 7 - RIGHT_HOPS[k]
@@ -63,8 +67,8 @@
     return high, middle, rest - middle
 
 
-def chain_kernel(a_hbm, g_hbm, e_hbm, w_hbm, m_ref, nx_ref, lx_ref,
-                 a_ref, e_ref, w_ref, g_all, we_ref,
+def chain_kernel(a_hbm, g_hbm, e_hbm, w_hbm, m_ref, nx_ref, lx_ref, ch_ref,
+                 a_ref, at_ref, e_ref, w_ref, g_all, we_ref,
                  p_send, p_buf, l_pair, l_send, l_buf, z_send, z_buf, r_pair, r_send, r_buf, n_send, n_buf,
                  load_sem, g_ssem, g_rsem, z_ssem, z_rsem, d_ssem, d_rsem, pair_ssem, pair_rsem):
     t = lax.axis_index("tensor")
@@ -116,9 +120,13 @@
                 else:
                     g_recv(d, s, k)
 
-    def z_exchange(i, send_of, buf):
-        for k in (4, 5, 3, 6, 2, 7, 1):
+    def z_exchange(i, send_of, buf, prepare=None):
+        for n, k in enumerate((4, 5, 3, 6, 2, 7, 1)):
             to = lax.rem(t + k, NZ)
+            if prepare is not None:
+                prepare(to)
+                if n in (2, 4):
+                    gather("prepare%d" % n)
             pltpu.make_async_remote_copy(send_of(to), buf.at[t], z_ssem.at[i], z_rsem.at[i],
                                          device_id={"tensor": to}, device_id_type=MESH).start()
 
@@ -145,9 +153,9 @@
     load_g.wait()
     g_own = g_all[pl.ds(pl.multiple_of(t * 32, 32), 32), :]
     p = fold(dot(we_ref[...], g_own, NT))
-    wide = jnp.concatenate([p] * NZ, axis=1)
-    lane = lax.broadcasted_iota(jnp.int32, (4, 256), 1)
-    wide = jnp.where(lane // 32 == t, wide, 0.0)
+    wide = jnp.concatenate([p] * 4, axis=1)
+    lane = lax.broadcasted_iota(jnp.int32, (4, 128), 1)
+    wide = jnp.where(lane // 32 == lax.rem(t, 4), wide, 0.0)
     p_send[...] = wide
     p_buf[t] = wide
 
@@ -161,14 +169,15 @@
     for c in range(NZ):
         cols = pl.ds(c * COLS, COLS)
         left_e = left_e + dot(we_ref[:, cols], e_ref[:, cols], NT)
+        if c == 3:
+            gather("middle")
     load_a.wait()
+    at_ref[...] = jnp.transpose(a_ref[...])
 
     gather("left")
 
     z_wait(0, p_buf)
-    p_all = p_buf[0]
-    for i in range(1, NZ):
-        p_all = p_all + p_buf[i]
+    p_all = jnp.concatenate([p_buf[0] + p_buf[1] + p_buf[2] + p_buf[3], p_buf[4] + p_buf[5] + p_buf[6] + p_buf[7]], axis=1)
     left_part = fold(left_e) + fold(dot(split16(p_all), a_ref[...], NN))
     l_pair[0] = left_part
     pair_copy(0, l_pair.at[0], l_pair.at[1]).start()
@@ -185,18 +194,20 @@
     for i in range(1, CHIPS):
         lm = lm + l_buf[i]
     lm = lm * (1.0 / DP)
-    peak = jnp.maximum(jnp.max(jnp.max(jnp.abs(lm), axis=1, keepdims=True), axis=0, keepdims=True), 1e-30)
-    lm = lm / peak
+    peak = jnp.maximum(jnp.max(jnp.abs(lm), axis=1, keepdims=True), 1e-30)
+    lm = lm * (1.0 / peak)
     l16 = split16(lm)
     gram = fold(dot(l16, l16, NT))
     gram = gram[:, 0:4] + gram[:, 4:8] + gram[:, 8:12]
     info = jnp.concatenate([gram, jnp.broadcast_to(peak, (4, 124))], axis=1)
     q = fold(dot(l16, a_ref[...], NT))
-    for c in range(NZ):
-        z_send[c, :, 640:896] = q
-        z_send[c, :, 896:1024] = info
-        z_send[c, :, 0:640] = fold(dot(l16, e_ref[:, c * COLS:(c + 1) * COLS], NN))
-    z_exchange(1, lambda to: z_send.at[to], z_buf)
+    def prepare(to):
+        z_send[to, :, 640:896] = q
+        z_send[to, :, 896:1024] = info
+        z_send[to, :, 0:640] = fold(dot(l16, e_ref[:, pl.ds(pl.multiple_of(to * COLS, COLS), COLS)], NN))
+
+    z_exchange(1, lambda to: z_send.at[to], z_buf, prepare)
+    prepare(t)
     z_buf[t] = z_send[t]
 
     gather("sums")
@@ -206,12 +217,11 @@
     top = peaks[0]
     for i in range(1, NZ):
         top = jnp.maximum(top, peaks[i])
-    scales = [x / top for x in peaks]
+    inv = 1.0 / top
+    scales = [x * inv for x in peaks]
     total = z_buf[0, :, 0:896] * scales[0]
-    gram = z_buf[0, :, 896:900] * (scales[0] * scales[0])
     for i in range(1, NZ):
         total = total + z_buf[i, :, 0:896] * scales[i]
-        gram = gram + z_buf[i, :, 896:900] * (scales[i] * scales[i])
     gather("mine")
     mine = pl.ds(pl.multiple_of(t * COLS, COLS), COLS)
     right_part = total[:, 0:640] + fold(dot(split16(total[:, 640:896]), g_all[:, mine], NN))
@@ -224,29 +234,40 @@
     r_buf[chip] = right_part
     dp_exchange(1, r_send, r_buf)
 
+    diagonal = lax.broadcasted_iota(jnp.int32, (4, 4), 0) == lax.broadcasted_iota(jnp.int32, (4, 4), 1)
+    gram = jnp.zeros((4, 4), F32)
+    for i in range(NZ):
+        across = jnp.sum(jnp.where(diagonal, scales[i], 0.0), axis=0, keepdims=True)
+        gram = gram + z_buf[i, :, 896:900] * scales[i] * across
     lower = [[None] * 4 for _ in range(4)]
+    inverse = [None] * 4
     for i in range(4):
         for j in range(i + 1):
             v = gram[i:i + 1, j:j + 1]
             for k in range(j):
                 v = v - lower[i][k] * lower[j][k]
-            lower[i][j] = jnp.sqrt(v) if i == j else v / lower[j][j]
-
-    def solve(rows):
-        out = []
-        for j in range(4):
-            v = rows[j]
-            for i in range(j):
-                v = v - out[i] * lower[j][i]
-            out.append(v / lower[j][j])
-        return jnp.concatenate(out, axis=0)
-
-    own_scale = peak / top[0:1]
-    lm = lm * own_scale
-    lo = solve([lm[j:j + 1] for j in range(4)])
-    high, middle, low = parts3(lo)
-    zero = jnp.zeros_like(lo)
+            lower[i][j] = jnp.sqrt(v) if i == j else v * inverse[j]
+        inverse[i] = 1.0 / lower[i][i]
+
+    rows = lm * (peak * inv)
+    lo = []
+    for j in range(4):
+        v = rows[j:j + 1]
+        for i in range(j):
+            v = v - lo[i] * lower[j][i]
+        lo.append(v * inverse[j])
+    both = [None] * 4
+    for j in (3, 2, 1, 0):
+        v = lo[j]
+        for i in range(j + 1, 4):
+            v = v - both[i] * lower[i][j]
+        both[j] = v * inverse[j]
+    high, middle, low = parts3(jnp.concatenate(both, axis=0))
+    zero = jnp.zeros_like(high)
     lx_ref[...] = jnp.concatenate([high, high, middle, middle, high, low, zero, zero], axis=0).astype(BF)
+    flat = [lower[i][j] if i != j else inverse[i] for i in range(4) for j in range(4) if j <= i]
+    for i, v in enumerate(flat):
+        ch_ref[i:i + 1, :] = jnp.broadcast_to(v, (1, 128))
 
     gather("sent1")
     dp_wait(1, r_buf)
@@ -260,33 +281,34 @@
 
     gather("rest")
 
-    at = jnp.transpose(a_ref[...])
-    for c in range(NZ):
-        cols = slice(c * COLS, (c + 1) * COLS)
-        m_ref[:, cols] = dot(at, g_all[:, cols], NN) + e_ref[:, cols].astype(F32)
-
-    z_wait(2, n_buf)
-    for c in range(NZ):
-        x = n_buf[c]
-        nx_ref[:, c * COLS:(c + 1) * COLS] = solve([x[j:j + 1] for j in range(4)])
+    def matrix(chunk):
+        cols = pl.ds(pl.multiple_of(lax.rem(chunk, NZ) * COLS, COLS), COLS)
+        m_ref[:, cols] = dot(at_ref[...], g_all[:, cols], NN) + e_ref[:, cols].astype(F32)
+
+    matrix(t)
+    for d, k in ((0, 3), (1, 5), (0, 2), (1, 6), (0, 1), (1, 7), (1, 0)):
+        g_recv(d, 3, k)
+        matrix(t + 4 + k)
 
     for d in range(2):
         for k in range(NZ):
             for s in range(hops(d, k)):
                 g_copy(d, s, k).wait_send()
-    for i, buf in enumerate((p_buf, z_buf, n_buf)):
-        w = buf.at[pl.ds(0, NZ - 1)]
-        pltpu.make_async_copy(w, w, z_ssem.at[i]).wait()
     pair_copy(0, l_pair.at[0], l_pair.at[1]).wait_send()
     pair_copy(1, r_pair.at[0], r_pair.at[1]).wait_send()
     for i, buf in enumerate((l_buf, r_buf)):
         w = buf.at[pl.ds(0, CHIPS - 1)]
         pltpu.make_async_copy(w, w, d_ssem.at[i]).wait()
-
-
-def finish_kernel(m_ref, n_ref, lx_ref, rebuilt_hbm, error_hbm, nout_ref, out_a, out_b, sem):
+    for i, buf in enumerate((p_buf, z_buf, n_buf)):
+        w = buf.at[pl.ds(0, NZ - 1)]
+        pltpu.make_async_copy(w, w, z_ssem.at[i]).wait()
+    z_wait(2, n_buf)
+    for c in range(NZ):
+        nx_ref[:, c * COLS:(c + 1) * COLS] = n_buf[c]
+
+
+def finish_kernel(m_ref, n_ref, lx_ref, ch_ref, rebuilt_hbm, error_hbm, nout_ref, out_a, out_b, sem):
     lxt = lx_ref[...]
-    nout_ref[...] = n_ref[...]
     copies = []
     for c in range(NZ):
         cols = slice(c * COLS, (c + 1) * COLS)
@@ -300,6 +322,14 @@
             cp = pltpu.make_async_copy(src.at[:, cols], dst.at[:, cols], sem.at[i, c])
             cp.start()
             copies.append(cp)
+    ch = [ch_ref[i:i + 1, 0:1] for i in range(10)]
+    out = []
+    for j in range(4):
+        v = n_ref[j:j + 1, :]
+        for i in range(j):
+            v = v - out[i] * ch[j * (j + 1) // 2 + i]
+        out.append(v * ch[j * (j + 1) // 2 + j])
+        nout_ref[j:j + 1, :] = out[j]
     for cp in copies:
         cp.wait()
 
@@ -310,14 +340,14 @@
     vmem = pl.BlockSpec(memory_space=pltpu.VMEM)
     V = pltpu.VMEM
     D = pltpu.SemaphoreType.DMA
-    m, n, lx = pl.pallas_call(
+    m, n, lx, ch = pl.pallas_call(
         chain_kernel,
         out_shape=OUT_SHAPES(),
         in_specs=[hbm_spec] * 4,
-        out_specs=[vmem] * 3,
+        out_specs=[vmem] * 4,
         scratch_shapes=[
-            V((256, 384), BF), V((384, 5120), BF), V((4, 5120), F32), V((256, 5120), BF), V((16, 5120), BF),
-            V((4, 256), F32), V((NZ, 4, 256), F32), V((2, 4, 384), F32), V((4, 384), F32), V((CHIPS, 4, 384), F32),
+            V((256, 384), BF), V((384, 256), BF), V((384, 5120), BF), V((4, 5120), F32), V((256, 5120), BF), V((16, 5120), BF),
+            V((4, 128), F32), V((NZ, 4, 128), F32), V((2, 4, 384), F32), V((4, 384), F32), V((CHIPS, 4, 384), F32),
             V((NZ, 4, 1024), F32), V((NZ, 4, 1024), F32), V((2, 4, 640), F32), V((4, 640), F32), V((CHIPS, 4, 640), F32),
             V((4, 640), F32), V((NZ, 4, 640), F32),
             D((4,)), D((2, 4, NZ)), D((2, 4, NZ)), D((3,)), D((3,)), D((2,)), D((2,)), D((2,)), D((2,)),
@@ -329,17 +359,17 @@
         finish_kernel,
         out_shape=[jax.ShapeDtypeStruct((384, 5120), BF), jax.ShapeDtypeStruct((384, 5120), BF),
                    jax.ShapeDtypeStruct((4, 5120), F32)],
-        in_specs=[vmem] * 3,
+        in_specs=[vmem] * 4,
         out_specs=[any_spec, any_spec, vmem],
         scratch_shapes=[V((384, 5120), BF), V((384, 5120), BF), D((2, NZ))],
         compiler_params=pltpu.CompilerParams(vmem_limit_bytes=32 << 20),
-    )(m, n, lx)
+    )(m, n, lx, ch)
     return rebuilt, error[None], factor.T
 
 
 def OUT_SHAPES():
     return [jax.ShapeDtypeStruct((384, 5120), F32), jax.ShapeDtypeStruct((4, 5120), F32),
-            jax.ShapeDtypeStruct((32, 384), BF)]
+            jax.ShapeDtypeStruct((32, 384), BF), jax.ShapeDtypeStruct((16, 128), F32)]
 
 
 def solution(mesh):

time: 48.4 us -> 47.9 us (0.990)
  Pallas kernels: 47.7 us -> 47 us
    pallas_call x1, Pallas kernels: 43.5 us -> 42.8 us  [per_device(): pl.pallas_call(chain_kernel, out_shape=OUT_SHAPES(), in_specs=[hbm_spec]...]
where the time goes in v3:
time: 47.9 us; the launch traced here: 47.6 us
  Pallas kernels  47 us (98%)
  between operations  0.64 us (1%)
    pallas_call x1, Pallas kernels, per_device(): pl.pallas_call(chain_kernel, out_shape=OUT_SHAPES(), in_specs=[hbm_spec]...  42.8 us
    pallas_call x1, Pallas kernels, per_device(): pl.pallas_call(finish_kernel, out_shape=[jax.ShapeDtypeStruct((384, 5120)...  4.24 us

profile of v3, /device:TPU:32, one launch (start us, length us, event | category | flops | bytes accessed | tf_op | source)
XLA Modules:
  0.0 47.6 jit_solution(6022587981995517871)
XLA Ops:
  0.6 42.8 %shard_map.67 = (f32[384,5120]{1,0:T(8,128)S(1)}, f32[4,5120]{1,0:T(4,128)S(1)}, bf16[32,384]{1,0:T(8,128)(2,1)S(1)}, f32[16,128]{1,0:T(8,128)S(1)}) custom-call(bf16[256,384]{1,0:T(8,128)(2,1)} %bitcast.8, bf16[32,5120]{1,0:T(8,128)(2,1)} %bitcast.7, bf16[384,5120]{1,0:T(8,128)(2,1)} %bitcast.6, f32[4,5120]{1,0:T(4,128)} %bitcast.9), custom_call_target="tpu_custom_call" | custom-call | tf_op jit(solution)/shard_map/pallas_call | solution.py:343
  43.4 4.2 %shard_map.68 = (bf16[384,5120]{1,0:T(8,128)(2,1)}, bf16[384,5120]{1,0:T(8,128)(2,1)}, f32[4,5120]{1,0:T(4,128)}) custom-call(f32[384,5120]{1,0:T(8,128)S(1)} %get-tuple-element.10.m_ref, f32[4,5120]{1,0:T(4,128)S(1)} %get-tuple-element.11.n_ref, bf16[32,384]{1,0:T(8,128)(2,1)S(1)} %get-tuple-element.12.lx_ref, f32[16,128]{1,0:T(8,128)S(1)} %get-tuple-element.13.ch_ref), custom_call_target="tpu_custom_call" | custom-call | tf_op jit(solution)/shard_map/pallas_call | solution.py:358

commit v4 on v3

--- a/solution.py
+++ b/solution.py
@@ -26,13 +26,13 @@
     "middle": (),
     "left": ((0, 0, (4, 3, )), (1, 0, (5, ))),
     "pair0": ((0, 0, (2, )), (1, 0, (6, )), (0, -1, (6, 5, )), (1, -1, (2, 1, ))),
-    "sent0": ((0, 1, (4, 3, )), (1, 1, (5, )), (0, 0, (1, 0, )), (1, 0, (7, 0, ))),
+    "sent0": ((0, 1, (4, 3, )), (1, 1, (5, )), (0, 0, (1, 0, 7, )), (1, 0, (7, 0, 4, ))),
     "prepare2": (),
     "prepare4": (),
-    "sums": ((0, 2, (4, )), (0, 0, (7, 6, 5, )), (1, 0, (4, 3, 2, 1, )), (0, 1, (2, 1, )), (1, 1, (6, 7, ))),
-    "mine": ((0, 3, (4, )), (0, 2, (3, )), (1, 2, (5, )), (0, 1, (0, )), (1, 1, (0, ))),
-    "pair1": ((0, 1, (7, )), (1, 1, (4, ))),
-    "sent1": ((0, 1, (6, 5, )), (1, 1, (3, 2, 1, )), (0, 2, (2, 1, )), (1, 2, (6, 7, 0, ))),
+    "sums": ((0, 2, (4, )), (0, 0, (6, 5, )), (1, 0, (3, 2, 1, )), (0, 1, (2, 1, )), (1, 1, (6, 7, ))),
+    "mine": ((0, 3, (4, )), (0, 2, (3, )), (1, 2, (5, ))),
+    "pair1": ((0, 1, (0, 7, 6, )), (1, 1, (0, 4, 3, ))),
+    "sent1": ((0, 1, (5, )), (1, 1, (2, 1, )), (0, 2, (2, 1, )), (1, 2, (6, 7, 0, ))),
     "rest": ((0, 2, (0, 7, 6, 5, )), (1, 2, (4, 3, 2, 1, ))),
 }
 

time: 47.9 us -> 48 us (level)
  no operation moved by 1% of the time
where the time goes in v4:
time: 48 us
  Pallas kernels  47.3 us (99%)
  between operations  0.64 us (1%)
    pallas_call x1, Pallas kernels, per_device(): pl.pallas_call(chain_kernel, out_shape=OUT_SHAPES(), in_specs=[hbm_spec]...  43.1 us
    pallas_call x1, Pallas kernels, per_device(): pl.pallas_call(finish_kernel, out_shape=[jax.ShapeDtypeStruct((384, 5120)...  4.25 us

profile of v4, /device:TPU:32, one launch (start us, length us, event | category | flops | bytes accessed | tf_op | source)
XLA Modules:
  0.0 48.0 jit_solution(5777488866052295604)
XLA Ops:
  0.6 43.1 %shard_map.67 = (f32[384,5120]{1,0:T(8,128)S(1)}, f32[4,5120]{1,0:T(4,128)S(1)}, bf16[32,384]{1,0:T(8,128)(2,1)S(1)}, f32[16,128]{1,0:T(8,128)S(1)}) custom-call(bf16[256,384]{1,0:T(8,128)(2,1)} %bitcast.8, bf16[32,5120]{1,0:T(8,128)(2,1)} %bitcast.7, bf16[384,5120]{1,0:T(8,128)(2,1)} %bitcast.6, f32[4,5120]{1,0:T(4,128)} %bitcast.9), custom_call_target="tpu_custom_call" | custom-call | tf_op jit(solution)/shard_map/pallas_call | solution.py:343
  43.7 4.2 %shard_map.68 = (bf16[384,5120]{1,0:T(8,128)(2,1)}, bf16[384,5120]{1,0:T(8,128)(2,1)}, f32[4,5120]{1,0:T(4,128)}) custom-call(f32[384,5120]{1,0:T(8,128)S(1)} %get-tuple-element.10.m_ref, f32[4,5120]{1,0:T(4,128)S(1)} %get-tuple-element.11.n_ref, bf16[32,384]{1,0:T(8,128)(2,1)S(1)} %get-tuple-element.12.lx_ref, f32[16,128]{1,0:T(8,128)S(1)} %get-tuple-element.13.ch_ref), custom_call_target="tpu_custom_call" | custom-call | tf_op jit(solution)/shard_map/pallas_call | solution.py:358
